TPU v7x, 32 devices: a whole 2x2x4 slice. The times are simulated.
32 devices in a mesh: gx: 8 (over z, x), gy: 4 (over y, core).
Axes of the slice: x: 2, y: 2, z: 4, core: 2. Of those that a mesh axis runs over, the one named last changes fastest.
Arguments:
- field_in: bfloat16 [20, 32, 128, 1024], P(None, 'gx', 'gy'), may hold values from -6 to 6
- cotangent: bfloat16 [20, 32, 128, 1024], P(None, 'gx', 'gy'), may hold values from -6 to 6
- spec_weight: float32 [2, 192, 20, 20, 24, 24], P(None, 'gx', None, None, 'gy'), may hold values from -6 to 6
Outputs:
- grad_field: bfloat16 [20, 32, 128, 1024], P(None, 'gx', 'gy')
- grad_weight: float32 [2, 192, 20, 20, 24, 24], P(None, 'gx', None, None, 'gy')
All inputs are finite; a program needn't handle non-finite values.
Results may differ from a plain program's by a relative error of at most 0.001.
Values sent between devices are 32-bit elements; how exact they have to be, the bound alone decides.
A program may use at most 512 MiB of HBM per device.

v0:
```python
import math

import jax
import jax.numpy as jnp
from jax import lax
from jax.sharding import PartitionSpec as P

MX = 12
MY = 12
MZ = 12
MT = 8
Z = 64
T_SIZE = 16
KX = 24
KY = 24
M = 192


exact_precision = lax.Precision.HIGHEST
split_precision = lax.Precision.HIGH
lead_contract = (((0,), (0,)), ((), ()))
tail_contract = (((1,), (1,)), ((), ()))


def signed_freqs(count, half_count):
    ladder = lax.iota(jnp.int32, count)
    return jnp.where(ladder < half_count, ladder, ladder - 2 * half_count)


def pair_table(frequencies, length):
    places = lax.iota(jnp.int32, length)
    residue = jnp.remainder(frequencies[:, None] * places[None, :], length)
    phases = residue.astype(jnp.float32) * (2.0 * math.pi / length)
    cosine = jnp.cos(phases) / math.sqrt(length)
    sines = jnp.sin(phases) / math.sqrt(length)
    return jnp.stack([jnp.stack([cosine, sines]), jnp.stack([-sines, cosine])])


def depth_rows_table():
    cell_ids = lax.iota(jnp.int32, Z * T_SIZE)
    depth_index = cell_ids // T_SIZE
    time_index = cell_ids % T_SIZE
    mode_ids = lax.iota(jnp.int32, M)
    depth_freq = mode_ids // MT
    depth_freq = jnp.where(depth_freq < MZ, depth_freq, depth_freq - 2 * MZ)
    time_freq = mode_ids % MT
    residue = jnp.remainder(
        depth_freq[:, None] * depth_index[None, :] * T_SIZE
        + time_freq[:, None] * time_index[None, :] * Z,
        Z * T_SIZE,
    )
    phases = residue.astype(jnp.float32) * (2.0 * math.pi / (Z * T_SIZE))
    factor = 1.0 / math.sqrt(Z * T_SIZE)
    return jnp.stack([jnp.cos(phases) * factor, -jnp.sin(phases) * factor])


def split_table(table):
    leading = table.astype(jnp.bfloat16)
    residual_part = (table - lax.optimization_barrier(leading).astype(jnp.float32)).astype(
        jnp.bfloat16
    )
    return (leading, residual_part)


def per_device(field_in, cotangent, spec_weight):
    channels, x_local, y_local, depth_time = field_in.shape
    x_groups = lax.axis_size("gx")
    x_count = x_local * x_groups
    y_count = y_local * lax.axis_size("gy")
    mode_local = M // x_groups
    x_table = pair_table(signed_freqs(KX, MX), x_count)
    x_blocks = x_table.reshape(2, 2, KX, x_groups, x_local)
    y_table = pair_table(signed_freqs(KY, MY), y_count)
    depth_modes = depth_rows_table()
    depth_flat = depth_modes.reshape(2 * M, depth_time)
    depth_lead, depth_tail = split_table(depth_flat)

    def depth_forward(flat_rows):
        first = lax.dot_general(
            depth_lead, flat_rows, tail_contract, preferred_element_type=jnp.float32
        )
        return first + lax.dot_general(
            depth_tail, flat_rows, tail_contract, preferred_element_type=jnp.float32
        )

    spectra = jnp.stack(
        [
            depth_forward(field_in.reshape(-1, depth_time)),
            depth_forward(cotangent.reshape(-1, depth_time)),
        ]
    ).reshape(2, 2, x_groups, mode_local, channels, x_local * y_local)
    section = lax.all_to_all(spectra, "gx", split_axis=2, concat_axis=2, tiled=True)
    planes = section.reshape(section.shape[:5] + (x_local, y_local))
    regrouped = jnp.einsum("pqkbx,fqbjcxy->fpjcky", x_blocks, planes, precision=exact_precision)
    at_modes = jnp.einsum(
        "pqky,fqjcay->fpjcak",
        y_table,
        lax.all_to_all(regrouped, "gy", split_axis=4, concat_axis=5, tiled=True),
        precision=exact_precision,
    )
    mode_ids = lax.axis_index("gx") * mode_local + lax.iota(jnp.int32, mode_local)
    doubling = jnp.where(mode_ids % MT == 0, 1.0, 2.0).astype(jnp.float32)[:, None, None, None]
    field_real = at_modes[0, 0]
    field_imag = at_modes[0, 1]
    dual_real = at_modes[1, 0] * doubling
    dual_imag = at_modes[1, 1] * doubling
    grad_real = (
        field_real[:, :, None] * dual_real[:, None] + field_imag[:, :, None] * dual_imag[:, None]
    )
    grad_imag = (
        field_real[:, :, None] * dual_imag[:, None] - field_imag[:, :, None] * dual_real[:, None]
    )
    grad_weight = jnp.stack([grad_real, grad_imag])
    back_real = jnp.sum(
        spec_weight[0] * dual_real[:, None] + spec_weight[1] * dual_imag[:, None], axis=2
    )
    back_imag = jnp.sum(
        spec_weight[0] * dual_imag[:, None] - spec_weight[1] * dual_real[:, None], axis=2
    )
    backward = jnp.stack([back_real, back_imag])
    spread = jnp.einsum("qpky,qjcak->pjcay", y_table, backward, precision=exact_precision)
    y_done = lax.all_to_all(spread, "gy", split_axis=4, concat_axis=3, tiled=True)
    x_spread = jnp.einsum("qpkbx,qjcky->pjcbxy", x_blocks, y_done, precision=exact_precision)
    section = lax.all_to_all(x_spread, "gx", split_axis=3, concat_axis=1, tiled=True)
    rows = section.reshape(section.shape[0] * section.shape[1], -1)
    summed = lax.dot_general(rows, depth_flat, lead_contract, precision=split_precision)
    grad_field = summed.reshape(section.shape[2], x_local, y_local, depth_time)
    return (grad_field.astype(jnp.bfloat16), grad_weight)


def solution(mesh):
    in_specs = (
        P(None, "gx", "gy", None),
        P(None, "gx", "gy", None),
        P(None, "gx", None, None, "gy", None),
    )
    out_specs = (P(None, "gx", "gy", None), P(None, "gx", None, None, "gy", None))
    return jax.shard_map(
        per_device, mesh=mesh, in_specs=in_specs, out_specs=out_specs, check_vma=False
    )
```

profile of v0, /device:TPU:0, one launch (start us, length us, event | category | flops | bytes accessed | tf_op | source)
XLA Modules:
  0.0 973.2 jit_solution(12397050707754505371)
XLA Ops:
  50.7 171.6 %all-to-all-done = f32[2,2,8,24,20,128]{5,3,4,1,0,2:T(8,128)} async-done(((f32[2,2,8,24,20,128]{5,3,4,1,0,2:T(8,128)}), f32[2,2,8,24,20,128]{5,3,4,1,0,2:T(8,128)}, u32[]{:S(2)}, u32[]{:S(2)}) %all-to-all-start) | async-done | bytes 7864352 | tf_op jit(solution)/shard_map/all_to_all | solution.py:92
  222.3 22.2 %reshape.638 = f32[2,2,8,24,20,4,32]{6,5,3,4,1,0,2:T(4,128)} reshape(f32[2,2,8,24,20,128]{5,3,4,1,0,2:T(8,128)} %all-to-all-done) | data formatting | bytes 15728640 | tf_op jit(solution)/shard_map/reshape | solution.py:93
  244.5 45.4 %fusion.11 = f32[2,2,24,20,24,32]{5,4,1,3,2,0:T(8,128)} fusion(f32[1,1,24,8,4]{2,4,1,3,0:T(4,128)S(1)} %get-tuple-element.16, f32[1,1,24,8,4]{2,4,1,3,0:T(4,128)S(1)} %get-tuple-element.15, f32[1,1,24,8,4]{2,4,1,3,0:T(4,128)S(1)} %get-tuple-element.14, f32[2,2,8,24,20,4,32]{6,5,3,4,1,0,2:T(4,128)} %reshape.638), kind=kOutput, calls=%fused_computation.17 | convolution fusion | flops 1132471296 | bytes 13771776 | tf_op jit(solution)/shard_map/pqkbx,fqbjcxy->fpjcky/dot_general | solution.py:94
  290.0 33.4 %copy.88 = f32[2,2,24,20,24,32]{5,1,3,2,0,4:T(2,128)} copy(f32[2,2,24,20,24,32]{5,4,1,3,2,0:T(8,128)} %fusion.11) | data formatting | bytes 11796480 | tf_op jit(solution)/shard_map/pqkbx,fqbjcxy->fpjcky/transpose | solution.py:94
  323.4 38.0 %reshape.640 = f32[4,1,368640]{2,1,0:T(1,128)} reshape(f32[24,2,24,20,2,32]{5,4,3,2,1,0:T(2,128)} %bitcast.149) | data formatting | bytes 11796480
  366.7 66.3 %all-to-all-done.1 = f32[4,1,368640]{2,1,0:T(1,128)} async-done(((f32[4,1,368640]{2,1,0:T(1,128)}), f32[4,1,368640]{2,1,0:T(1,128)}, u32[]{:S(2)}, u32[]{:S(2)}) %all-to-all-start.1) | async-done | bytes 5898272 | tf_op jit(solution)/shard_map/all_to_all | solution.py:98
  433.6 40.2 %reduce = f32[4,368640]{1,0:T(4,128)} reduce(f32[4,1,368640]{2,1,0:T(1,128)} %all-to-all-done.1, f32[]{:T(128)} %broadcast.886), dimensions={1}, to_apply=%all_to_all.41.reduce_sub_computation | reduce | bytes 11796484 | tf_op jit(solution)/shard_map/all_to_all | solution.py:98
  473.8 40.6 %reshape.641 = f32[24,2,24,20,2,32]{5,4,3,2,1,0:T(2,128)} reshape(f32[4,368640]{1,0:T(4,128)} %reduce) | data formatting | bytes 11796480
  514.4 12.9 %copy.39 = f32[2,2,24,20,24,32]{5,2,4,3,1,0:T(8,128)S(1)} copy(f32[2,2,24,20,24,32]{5,1,3,2,0,4:T(2,128)} %bitcast.150) | data formatting | bytes 11796480 | tf_op jit(solution)/shard_map/all_to_all | solution.py:98
  537.7 18.4 %reshape.628 = f32[2,2,24,20,6,128,1]{5,2,1,4,3,0,6:T(8,128)} reshape(f32[2,2,24,20,6,4,32]{6,5,2,1,4,3,0:T(4,128)} %copy.40) | data formatting | bytes 11796480 | tf_op jit(solution)/shard_map/all_to_all | solution.py:98
  566.0 20.9 %fusion.3 = (f32[24,20,6,24]{3,0,2,1:T(8,128)S(1)}, f32[24,20,6,24]{3,0,2,1:T(8,128)S(1)}) fusion(f32[2,24,20,20,6,24]{5,1,4,3,2,0:T(8,128)} %param.5, f32[24,20,6,24]{3,0,2,1:T(8,128)S(1)} %get-tuple-element.5, f32[24,20,6,24]{3,0,2,1:T(8,128)S(1)} %get-tuple-element.4), kind=kLoop, calls=%fused_computation.6 | loop fusion | flops 10920960 | bytes 12165120 | tf_op jit(solution)/shard_map/reduce_sum | solution.py:114
  591.1 17.7 %copy.43 = f32[2,24,20,6,128]{1,0,3,2,4:T(2,128)} copy(f32[2,24,20,6,128]{4,1,0,3,2:T(8,128)} %fusion.24) | data formatting | bytes 5898240 | tf_op jit(solution)/shard_map/qpky,qjcak->pjcay/transpose | solution.py:121
  608.8 31.3 %reshape.642 = f32[4,1,184320]{2,1,0:T(1,128)} reshape(f32[128,20,6,2,24]{4,3,2,1,0:T(2,128)} %bitcast.153) | data formatting | bytes 5898240
  644.7 34.9 %all-to-all-done.2 = f32[4,1,184320]{2,1,0:T(1,128)} async-done(((f32[4,1,184320]{2,1,0:T(1,128)}), f32[4,1,184320]{2,1,0:T(1,128)}, u32[]{:S(2)}, u32[]{:S(2)}) %all-to-all-start.2) | async-done | bytes 2949152 | tf_op jit(solution)/shard_map/all_to_all | solution.py:122
  690.9 37.1 %reshape.643 = f32[128,20,6,2,24]{4,3,2,1,0:T(2,128)} reshape(f32[4,184320]{1,0:T(4,128)} %reduce.1) | data formatting | bytes 5898240
  727.9 23.1 %copy.70 = f32[2,24,20,6,4,32]{5,4,1,3,2,0:T(4,128)} copy(f32[2,24,20,6,4,32]{1,0,3,2,5,4:T(2,128)} %bitcast.154) | data formatting | bytes 5898240 | tf_op jit(solution)/shard_map/all_to_all | solution.py:122
  761.0 18.8 %fusion.8 = f32[2,24,20,8,4,32]{5,3,4,0,2,1:T(8,128)S(1)} fusion(f32[2,24,20,24,32,1,1]{4,1,3,2,0,6,5:T(8,128)} %bitcast.152, f32[2,2,24,8,4,1,1]{2,4,1,3,0,6,5:T(4,128)S(1)} %fusion.37), kind=kOutput, calls=%fused_computation.16 | convolution fusion | flops 566231040 | bytes 6893568 | tf_op jit(solution)/shard_map/qpkbx,qjcky->pjcbxy/dot_general | solution.py:123
  788.1 14.3 %reshape.644 = f32[8,1,122880]{2,1,0:T(1,128)} reshape(f32[8,24,20,2,4,32]{5,4,3,2,1,0:T(4,128)} %bitcast.155) | data formatting | bytes 7864320
  809.1 19.2 %multiply_add_fusion = (f32[1,24,20,20,6,24]{5,1,4,3,2,0:T(8,128)}, f32[1,24,20,20,6,24]{5,1,4,3,2,0:T(8,128)}) fusion(f32[24,20,6,24]{3,0,2,1:T(8,128)S(1)} %get-tuple-element.5, f32[24,20,6,24]{3,0,2,1:T(8,128)S(1)} %get-tuple-element.9, f32[24,20,6,24]{3,0,2,1:T(8,128)S(1)} %get-tuple-element.4, f32[24,20,6,24]{3,0,2,1:T(8,128)S(1)} %get-tuple-element.8), kind=kLoop, calls=%fused_computation.12 | loop fusion | flops 8294400 | bytes 12165120 | tf_op jit(solution)/shard_map/add | solution.py:108
  828.3 39.0 %pad_maximum_fusion = f32[2,24,20,20,6,24]{5,1,4,3,2,0:T(8,128)} fusion(f32[1,24,20,20,6,24]{5,1,4,3,2,0:T(8,128)} %get-tuple-element.7, f32[1,24,20,20,6,24]{5,1,4,3,2,0:T(8,128)} %get-tuple-element.6), kind=kLoop, calls=%fused_computation | loop fusion | flops 2764800 | bytes 22118400 | tf_op jit(solution)/shard_map/stack | solution.py:113
  867.3 27.4 %all-to-all-done.3 = f32[8,1,122880]{2,1,0:T(1,128)} async-done(((f32[8,1,122880]{2,1,0:T(1,128)}), f32[8,1,122880]{2,1,0:T(1,128)}, u32[]{:S(2)}, u32[]{:S(2)}) %all-to-all-start.3) | async-done | bytes 3932192 | tf_op jit(solution)/shard_map/all_to_all | solution.py:124
  894.7 13.1 %reduce.2 = f32[8,122880]{1,0:T(8,128)} reduce(f32[8,1,122880]{2,1,0:T(1,128)} %all-to-all-done.3, f32[]{:T(128)} %broadcast.886), dimensions={1}, to_apply=%all_to_all.49.reduce_sub_computation | reduce | bytes 7864324 | tf_op jit(solution)/shard_map/all_to_all | solution.py:124
  907.7 15.8 %reshape.645 = f32[8,24,20,2,4,32]{5,4,3,2,1,0:T(4,128)} reshape(f32[8,122880]{1,0:T(8,128)} %reduce.2) | data formatting | bytes 7864320
  939.4 16.3 %reshape.624 = f32[384,2560]{1,0:T(8,128)} reshape(f32[2,8,24,20,1,4,32]{6,5,3,2,1,0,4:T(4,128)} %copy.49) | data formatting | bytes 7864320 | tf_op jit(solution)/shard_map/reshape | solution.py:125
  (50 shorter events, 154.3 us)
Async XLA Ops:
  0.7 4.9 slice-start
  4.1 1.2 copy-start
  4.1 1.8 slice-start.1
  43.0 179.3 %all-to-all-start = ((f32[2,2,8,24,20,128]{5,3,4,1,0,2:T(8,128)}), f32[2,2,8,24,20,128]{5,3,4,1,0,2:T(8,128)}, u32[]{:S(2)}, u32[]{:S(2)}) async-start(f32[2,2,8,24,20,128]{5,3,4,1,0,2:T(8,128)} %copy.35), calls=%async_computation | async-start | bytes 15728640 | tf_op jit(solution)/shard_map/all_to_all | solution.py:92
  361.4 71.7 %all-to-all-start.1 = ((f32[4,1,368640]{2,1,0:T(1,128)}), f32[4,1,368640]{2,1,0:T(1,128)}, u32[]{:S(2)}, u32[]{:S(2)}) async-start(f32[4,1,368640]{2,1,0:T(1,128)} %reshape.640), calls=%async_computation.1 | async-start | bytes 11796480 | tf_op jit(solution)/shard_map/all_to_all | solution.py:98
  563.3 2.5 copy-start.2
  640.1 39.5 %all-to-all-start.2 = ((f32[4,1,184320]{2,1,0:T(1,128)}), f32[4,1,184320]{2,1,0:T(1,128)}, u32[]{:S(2)}, u32[]{:S(2)}) async-start(f32[4,1,184320]{2,1,0:T(1,128)} %reshape.642), calls=%async_computation.2 | async-start | bytes 5898240 | tf_op jit(solution)/shard_map/all_to_all | solution.py:122
  802.3 92.3 %all-to-all-start.3 = ((f32[8,1,122880]{2,1,0:T(1,128)}), f32[8,1,122880]{2,1,0:T(1,128)}, u32[]{:S(2)}, u32[]{:S(2)}) async-start(f32[8,1,122880]{2,1,0:T(1,128)} %reshape.644), calls=%async_computation.3 | async-start | bytes 7864320 | tf_op jit(solution)/shard_map/all_to_all | solution.py:124
  955.8 5.6 copy-start.1
where the time goes:
time: 983 us; the launch traced here: 973 us
  local copies, waits for them, and re-layouts  393 us (40%)
  waiting for transfers between devices  300 us (31%)
  other arithmetic  153 us (16%)
  matrix products  105 us (11%)
  starting transfers between devices  22 us (2%)
    unnamed x16, local copies, waits for them, and re-layouts  181 us
    all_to_all x1, waiting for transfers between devices, per_device(): lax.all_to_all(spectra, 'gx', split_axis=2, concat_axis=2, tiled=True)  172 us
    all_to_all x1, waiting for transfers between devices, per_device(): lax.all_to_all(regrouped, 'gy', split_axis=4, concat_axis=5, tiled=True)  66.3 us
    dot_general x1, matrix products, per_device(): jnp.einsum('pqkbx,fqbjcxy->fpjcky', x_blocks, planes, precision=exact_pre...  45.4 us
    all_to_all x4, local copies, waits for them, and re-layouts, per_device(): lax.all_to_all(regrouped, 'gy', split_axis=4, concat_axis=5, tiled=True)  42.3 us
    all_to_all x1, other arithmetic, per_device(): lax.all_to_all(regrouped, 'gy', split_axis=4, concat_axis=5, tiled=True)  40.2 us
    another operation x1, other arithmetic, per_device(): grad_weight = jnp.stack([grad_real, grad_imag])  39 us
    all_to_all x1, waiting for transfers between devices, per_device(): lax.all_to_all(spread, 'gy', split_axis=4, concat_axis=3, tiled=True)  34.9 us
  transfers between devices with their start and end apart: 4, of which 4 were waited for; matrix products, arithmetic and copies ran while one was open for 6% of the time, Pallas kernels for 0%

commit v1 on v0

v1 whole, which is shorter than its diff:
```python
import functools
import math

import jax
import jax.numpy as jnp
import ml_dtypes
import numpy as np
from jax import lax
from jax.experimental import pallas as pl
from jax.experimental.pallas import tpu as pltpu
from jax.sharding import PartitionSpec as P

MX = 12
MY = 12
MZ = 12
MT = 8
Z = 64
T_SIZE = 16
KX = 24
KY = 24
M = 192
VMEM_LIMIT = 56 * 1024 * 1024

minor_contract = (((1,), (1,)), ((), ()))
plain_contract = (((1,), (0,)), ((), ()))
lead_contract = (((0,), (0,)), ((), ()))


def signed(count, half):
    ladder = np.arange(count)
    return np.where(ladder < half, ladder, ladder - 2 * half)


def split(table):
    table = np.asarray(table, np.float32)
    high = table.astype(ml_dtypes.bfloat16)
    low = (table - high.astype(np.float32)).astype(ml_dtypes.bfloat16)
    return high, low


def pair_table(count, half, length):
    residue = (signed(count, half)[:, None] * np.arange(length)[None, :]) % length
    phases = residue * (2.0 * math.pi / length)
    cosine = np.cos(phases) / math.sqrt(length)
    sine = np.sin(phases) / math.sqrt(length)
    return np.stack([np.stack([cosine, sine]), np.stack([-sine, cosine])])


def depth_table():
    cells = np.arange(Z * T_SIZE)
    modes = np.arange(M)
    depth_freq = signed(2 * MZ, MZ)[modes // MT]
    residue = (
        depth_freq[:, None] * (cells // T_SIZE)[None, :] * T_SIZE
        + (modes % MT)[:, None] * (cells % T_SIZE)[None, :] * Z
    ) % (Z * T_SIZE)
    phases = residue * (2.0 * math.pi / (Z * T_SIZE))
    scale = 1.0 / math.sqrt(Z * T_SIZE)
    return np.concatenate([np.cos(phases) * scale, -np.sin(phases) * scale])


def y_blocks(y_count, y_groups, x_local):
    table = pair_table(KY, MY, y_count).reshape(2, 2, KY, y_groups, -1)
    full = np.einsum("pqkgy,xw->gqxypwk", table, np.eye(x_local))
    return full.reshape(y_groups, 2 * x_local * table.shape[-1], 2 * x_local * KY)


def x_blocks(x_count, x_groups):
    table = pair_table(KX, MX, x_count).reshape(2, 2, KX, x_groups, -1)
    full = np.einsum("pqksx,yw->sqxykpw", table, np.eye(KY))
    return full.reshape(x_groups, 2 * table.shape[-1] * KY, KX * 2 * KY)


def halves(values):
    high = values.astype(jnp.bfloat16)
    return high, (values - high.astype(jnp.float32)).astype(jnp.bfloat16)


def mul(a, b, contract):
    return lax.dot_general(a, b, contract, preferred_element_type=jnp.float32)


def product(values, high, low, contract):
    v_high, v_low = halves(values)
    return (
        mul(v_high, low, contract) + mul(v_low, high, contract) + mul(v_high, high, contract)
    )


def params():
    return pltpu.CompilerParams(vmem_limit_bytes=VMEM_LIMIT)


def whole(shape):
    return pl.BlockSpec(shape, lambda *_: (0,) * len(shape))


def zt_y_kernel(rows_m, order, f_ref, g_ref, table, wh, wl, out):
    cells = jnp.concatenate(
        [ref[0].reshape(-1, ref.shape[-1]) for ref in (f_ref, g_ref)], axis=0
    )
    doubled = mul(table[...], cells, minor_contract)
    spectrum = doubled[: 2 * M] + doubled[2 * M :]
    half = spectrum.shape[1] // 2
    both = jnp.concatenate(
        [
            jnp.concatenate([spectrum[:M, at : at + half], spectrum[M:, at : at + half]], axis=1)
            for at in (0, half)
        ],
        axis=0,
    )
    planes = product(both, wh[0], wl[0], plain_contract)
    joined = jnp.concatenate([planes[:M], planes[M:]], axis=1)
    if rows_m % 8 == 0:
        out[0, :, 0] = joined.reshape(-1, rows_m, joined.shape[-1])
    else:
        out[0, 0] = joined


def x_kernel(last, r_ref, wh, wl, out, acc):
    step = pl.program_id(0)
    width = wh.shape[1]
    share = out.shape[2] // 2

    @pl.when(step == 0)
    def _():
        acc[...] = jnp.zeros_like(acc)

    for field in range(2):
        acc[field] += product(
            r_ref[0, :, field * width : (field + 1) * width], wh[0], wl[0], plain_contract
        )

    @pl.when(step == last)
    def _():
        for g in range(out.shape[0]):
            for field in range(2):
                out[g, :, field * share : (field + 1) * share] = acc[
                    field, :, g * share : (g + 1) * share
                ]


def back_kernel(v_ref, w_ref, s_ref, out, left, dual):
    share = v_ref.shape[2] // 2
    channels, kx_local = s_ref.shape[2:4]

    @pl.when(pl.program_id(0) == 0)
    def _():
        def one(o, carry):
            row = v_ref[o] * w_ref[...]
            row = jnp.concatenate([row, jnp.zeros((row.shape[0], 128), jnp.float32)], axis=1)
            for k in range(kx_local):
                at = 2 * k * KY
                real, imag = row[:, at : at + 128], row[:, at + KY : at + KY + 128]
                left[0, 0, o, k] = real
                left[0, 1, o, k] = -imag
                left[1, 0, o, k] = imag
                left[1, 1, o, k] = real
                at += share
                dual[0, o, k] = row[:, at : at + 128]
                dual[1, o, k] = row[:, at + KY : at + KY + 128]
            return carry

        lax.fori_loop(0, v_ref.shape[0], one, 0)

    for k in range(kx_local):
        real = jnp.zeros(s_ref.shape[4:], jnp.float32)
        imag = jnp.zeros(s_ref.shape[4:], jnp.float32)
        for o in range(channels):
            d_real, d_imag = dual[0, o, k, :, :KY], dual[1, o, k, :, :KY]
            s_real, s_imag = s_ref[0, 0, o, k], s_ref[1, 0, o, k]
            real += s_real * d_real + s_imag * d_imag
            imag += s_real * d_imag - s_imag * d_real
        at = 2 * k * KY
        out[0, :, at : at + KY] = real
        out[0, :, at + KY : at + 2 * KY] = imag


def x_back_kernel(b_ref, wh, wl, out, held):
    share = b_ref.shape[2]

    @pl.when(pl.program_id(0) == 0)
    def _():
        for g in range(b_ref.shape[0]):
            held[:, g * share : (g + 1) * share] = b_ref[g]

    out[0] = product(held[...], wh[0], wl[0], minor_contract)


def y_zt_back_kernel(order, q_ref, th, tl, wh, wl, *rest):
    out = rest[-1]
    rows = q_ref[...].reshape(M, q_ref.shape[-1])
    planes = product(rows, wh[0], wl[0], minor_contract)
    half = planes.shape[1] // 2
    stacked = jnp.concatenate([planes[:, :half], planes[:, half:]], axis=0)
    cells = product(stacked, th[...], tl[...], lead_contract)
    out[0] = cells.reshape(out.shape[1:]).astype(out.dtype)


def per_device(field_in, cotangent, spec_weight):
    channels, x_local, y_local, depth_time = field_in.shape
    n = lax.axis_size("gx")
    groups = lax.axis_size("gy")
    x_count, y_count = x_local * n, y_local * groups
    m_local = M // n
    kx_local = KX // groups
    c_local = channels // groups
    width = 2 * x_local * KY
    share = kx_local * 2 * KY
    cells = x_local * y_local
    aligned = m_local % 8 == 0
    me = lax.axis_index("gy")

    t_high, t_low = split(depth_table())
    t_both = np.concatenate([t_high, t_low])
    y_high, y_low = split(y_blocks(y_count, groups, x_local))
    x_high, x_low = split(x_blocks(x_count, n))

    ladder = lax.iota(jnp.int32, 2 * c_local)

    def order_of(first, second):
        owners = jnp.where(ladder < c_local, first, second)
        ids = owners * c_local + ladder % c_local
        return jnp.concatenate([ids, me[None]]).astype(jnp.int32)

    near = order_of(me, me ^ 2)
    far = order_of(me ^ 1, me ^ 3)
    count = 2 * c_local

    def field_spec():
        return pl.BlockSpec((1, x_local, y_local, depth_time), lambda i, o: (o[i], 0, 0, 0))

    def y_spec():
        return pl.BlockSpec((1, 2 * cells, width), lambda i, o: (o[count], 0, 0))

    if aligned:
        block = pl.BlockSpec(
            (1, n, 1, m_local, 2 * width), lambda i, o: (i // c_local, 0, i % c_local, 0, 0)
        )
        shape = (2, n, c_local, m_local, 2 * width)
    else:
        block = pl.BlockSpec(
            (1, 1, M, 2 * width), lambda i, o: (i // c_local, i % c_local, 0, 0)
        )
        shape = (2, c_local, M, 2 * width)

    def forward(order):
        result = pl.pallas_call(
            functools.partial(zt_y_kernel, m_local),
            out_shape=jax.ShapeDtypeStruct(shape, jnp.float32),
            grid_spec=pltpu.PrefetchScalarGridSpec(
                num_scalar_prefetch=1,
                grid=(count,),
                in_specs=[field_spec(), field_spec()]
                + [whole((4 * M, depth_time))]
                + [y_spec(), y_spec()],
                out_specs=block,
            ),
            compiler_params=params(),
            cost_estimate=pl.CostEstimate(
                flops=count * 2 * (4 * 2 * M * depth_time * cells + 6 * M * 2 * cells * width),
                bytes_accessed=count * (4 * cells * depth_time + 8 * M * width),
                transcendentals=0,
            ),
        )(order, field_in, cotangent, t_both, y_high, y_low)
        if not aligned:
            result = result.reshape(2, c_local, n, m_local, 2 * width).transpose(0, 2, 1, 3, 4)
        return result

    swap_core = [(d, d ^ 1) for d in range(groups)]
    swap_y = [(d, d ^ 2) for d in range(groups)]

    away = forward(far)
    arrived = lax.ppermute(away, "gy", swap_core)
    kept = forward(near)
    passed = lax.ppermute(kept[1] + arrived[1], "gy", swap_y)
    summed = (kept[0] + arrived[0]) + passed

    section = lax.all_to_all(summed, "gx", split_axis=0, concat_axis=0, tiled=True)
    rows = c_local * m_local
    section = section.reshape(n, rows, 2 * width)
    x_spec = pl.BlockSpec((1, width, groups * share), lambda s: (s, 0, 0))
    at_kx = pl.pallas_call(
        functools.partial(x_kernel, n - 1),
        out_shape=jax.ShapeDtypeStruct((groups, rows, 2 * share), jnp.float32),
        grid=(n,),
        in_specs=[pl.BlockSpec((1, rows, 2 * width), lambda s: (s, 0, 0)), x_spec, x_spec],
        out_specs=whole((groups, rows, 2 * share)),
        scratch_shapes=[pltpu.VMEM((2, rows, groups * share), jnp.float32)],
        compiler_params=params(),
    )(section, x_high, x_low)
    modes = lax.all_to_all(at_kx, "gy", split_axis=0, concat_axis=0, tiled=True)
    modes = modes.reshape(channels, m_local, 2 * share)

    mode_ids = lax.axis_index("gx") * m_local + lax.iota(jnp.int32, m_local)
    doubling = jnp.where(mode_ids % MT == 0, 1.0, 2.0).astype(jnp.float32)
    lanes = lax.iota(jnp.int32, 2 * share)[None]
    doubling = jnp.where(lanes < share, 1.0, doubling[:, None])

    weights = jnp.transpose(spec_weight, (0, 2, 3, 4, 1, 5))
    unpacked = (channels, kx_local, m_local, 128)
    padded = 2 * channels * channels * kx_local * m_local * 128 * 4
    backward, left, dual = pl.pallas_call(
        back_kernel,
        out_shape=[
            jax.ShapeDtypeStruct((channels, m_local, share), jnp.float32),
            jax.ShapeDtypeStruct((2, 2) + unpacked, jnp.float32),
            jax.ShapeDtypeStruct((2,) + unpacked, jnp.float32),
        ],
        grid=(channels,),
        in_specs=[
            whole((channels, m_local, 2 * share)),
            whole((m_local, 2 * share)),
            pl.BlockSpec((2, 1, channels, kx_local, m_local, KY), lambda i: (0, i, 0, 0, 0, 0)),
        ],
        out_specs=[
            pl.BlockSpec((1, m_local, share), lambda i: (i, 0, 0)),
            whole((2, 2) + unpacked),
            whole((2,) + unpacked),
        ],
        compiler_params=params(),
        cost_estimate=pl.CostEstimate(flops=2 * padded, bytes_accessed=padded, transcendentals=0),
    )(modes, doubling, weights)

    spread = lax.all_to_all(
        backward.reshape(groups, rows, share), "gy", split_axis=0, concat_axis=0, tiled=True
    )
    left, dual = left[..., None, :, :, :KY], dual[:, None, None, ..., :KY]
    grad_weight = left[0] * dual[0] + left[1] * dual[1]
    grad_weight = jnp.transpose(grad_weight, (0, 4, 1, 2, 3, 5))

    planes = pl.pallas_call(
        x_back_kernel,
        out_shape=jax.ShapeDtypeStruct((n, rows, width), jnp.float32),
        grid=(n,),
        in_specs=[whole((groups, rows, share)), x_spec, x_spec],
        out_specs=pl.BlockSpec((1, rows, width), lambda s: (s, 0, 0)),
        scratch_shapes=[pltpu.VMEM((rows, groups * share), jnp.float32)],
        compiler_params=params(),
    )(spread, x_high, x_low)
    own = lax.all_to_all(planes, "gx", split_axis=0, concat_axis=0, tiled=True)
    own = own.reshape(n, c_local, m_local, width)
    crossed = lax.ppermute(own, "gy", swap_y)
    crossed, grad_weight = lax.optimization_barrier((crossed, grad_weight))
    pair = jnp.stack([own, crossed])
    other = lax.ppermute(pair, "gy", swap_core)

    def inverse(order, values, target):
        if aligned:
            spec = pl.BlockSpec(
                (1, n, 1, m_local, width), lambda i, o: (i // c_local, 0, i % c_local, 0, 0)
            )
        else:
            values = values.transpose(0, 2, 1, 3, 4).reshape(2, c_local, M, width)
            spec = pl.BlockSpec(
                (1, 1, M, width), lambda i, o: (i // c_local, i % c_local, 0, 0)
            )
        extra = [] if target is None else [target]
        return pl.pallas_call(
            y_zt_back_kernel,
            out_shape=jax.ShapeDtypeStruct(field_in.shape, jnp.bfloat16),
            grid_spec=pltpu.PrefetchScalarGridSpec(
                num_scalar_prefetch=1,
                grid=(count,),
                in_specs=[spec]
                + [whole((2 * M, depth_time))] * 2
                + [y_spec(), y_spec()]
                + [pl.BlockSpec(memory_space=pl.ANY)] * len(extra),
                out_specs=field_spec(),
            ),
            input_output_aliases={6: 0} if extra else {},
            compiler_params=params(),
            cost_estimate=pl.CostEstimate(
                flops=count * (6 * 2 * M * depth_time * cells + 6 * M * 2 * cells * width),
                bytes_accessed=count * (2 * cells * depth_time + 4 * M * width),
                transcendentals=0,
            ),
        )(order, values, t_high, t_low, y_high, y_low, *extra)

    grad_field = inverse(near, pair, None)
    grad_field = inverse(far, other, grad_field)
    return (grad_field, grad_weight)


def solution(mesh):
    in_specs = (
        P(None, "gx", "gy", None),
        P(None, "gx", "gy", None),
        P(None, "gx", None, None, "gy", None),
    )
    out_specs = (P(None, "gx", "gy", None), P(None, "gx", None, None, "gy", None))
    return jax.shard_map(
        per_device, mesh=mesh, in_specs=in_specs, out_specs=out_specs, check_vma=False
    )
```

time: 983 us -> 294 us (0.30)
  local copies, waits for them, and re-layouts: 393 us -> 21.8 us
  waiting for transfers between devices: 300 us -> 61.8 us
  other arithmetic: 153 us -> 29.6 us
  Pallas kernels: 0 us -> 115 us
  matrix products: 105 us -> 0 us
  blocking collectives: 0 us -> 52.9 us
  starting transfers between devices: 22 us -> 11.1 us
    all_to_all x4 -> x2, waiting for transfers between devices: 300 us -> 28.8 us  [the longest x1 15.1 us: per_device(): modes = lax.all_to_all(at_kx, 'gy', split_axis=0, concat_axis=0, tiled=True)]
    unnamed x16 -> x12, local copies, waits for them, and re-layouts: 181 us -> 3.47 us
    pallas_call x0 -> x7, Pallas kernels: none -> 115 us  [the longest x1 35.6 us: per_device(): pl.pallas_call(back_kernel, out_shape=[jax.ShapeDtypeStruct((channels, m_...]
    dot_general x9 -> x0, matrix products: 105 us -> none  [the longest x1 45.4 us: per_device(): jnp.einsum('pqkbx,fqbjcxy->fpjcky', x_blocks, planes, precision=exact_pre...]
    all_to_all x8 -> x3, local copies, waits for them, and re-layouts: 91.3 us -> 5.07 us  [the longest x1 2.43 us: per_device(): own = lax.all_to_all(planes, 'gx', split_axis=0, concat_axis=0, tiled=True)]
    all_to_all x3 -> x0, other arithmetic: 64.5 us -> none  [the longest x1 40.2 us: per_device(): lax.all_to_all(regrouped, 'gy', split_axis=4, concat_axis=5, tiled=True)]
    transpose x3 -> x0, local copies, waits for them, and re-layouts: 59.4 us -> none  [the longest x1 33.4 us: per_device(): jnp.einsum('pqkbx,fqbjcxy->fpjcky', x_blocks, planes, precision=exact_pre...]
    all_to_all x0 -> x2, blocking collectives: none -> 52.9 us  [the longest x1 40.9 us: per_device(): lax.all_to_all(summed, 'gx', split_axis=0, concat_axis=0, tiled=True)]
  transfers between devices with their start and end apart: 4 -> 6, of which waited for: 4 -> 3; matrix products, arithmetic and copies ran while one was open for 6% -> 11% of each run, Pallas kernels for 0% -> 10%
where the time goes in v1:
time: 294 us; the launch traced here: 293 us
  Pallas kernels  115 us (39%)
  waiting for transfers between devices  61.8 us (21%)
  blocking collectives  52.9 us (18%)
  other arithmetic  29.6 us (10%)
  local copies, waits for them, and re-layouts  21.8 us (7%)
  starting transfers between devices  11.1 us (4%)
    all_to_all x1, blocking collectives, per_device(): lax.all_to_all(summed, 'gx', split_axis=0, concat_axis=0, tiled=True)  40.9 us
    pallas_call x1, Pallas kernels, per_device(): pl.pallas_call(back_kernel, out_shape=[jax.ShapeDtypeStruct((channels, m_...  35.6 us
    ppermute x1, waiting for transfers between devices, per_device(): passed = lax.ppermute(kept[1] + arrived[1], 'gy', swap_y)  33 us
    pallas_call x2, Pallas kernels, forward(): pl.pallas_call(functools.partial(zt_y_kernel, m_local), out_shape=jax.Sha...  31.7 us
    pallas_call x2, Pallas kernels, inverse(): pl.pallas_call(y_zt_back_kernel, out_shape=jax.ShapeDtypeStruct(field_in....  28.4 us
    add x1, other arithmetic, per_device(): grad_weight = left[0] * dual[0] + left[1] * dual[1]  24.4 us
    all_to_all x1, waiting for transfers between devices, per_device(): modes = lax.all_to_all(at_kx, 'gy', split_axis=0, concat_axis=0, tiled=True)  15.1 us
    all_to_all x1, waiting for transfers between devices, per_device(): own = lax.all_to_all(planes, 'gx', split_axis=0, concat_axis=0, tiled=True)  13.7 us
  transfers between devices with their start and end apart: 6, of which 3 were waited for; matrix products, arithmetic and copies ran while one was open for 11% of the time, Pallas kernels for 10%

profile of v1, /device:TPU:0, one launch (start us, length us, event | category | flops | bytes accessed | tf_op | source)
XLA Modules:
  0.0 292.8 jit_solution(15965714824736437974)
XLA Ops:
  1.3 15.8 %shard_map.114 = f32[2,8,5,24,384]{4,3,2,1,0:T(8,128)} custom-call(s32[11]{0:T(128)} %pad_add_fusion.order, bf16[20,4,32,1024]{3,2,1,0:T(8,128)(2,1)} %f_ref.3, bf16[20,4,32,1024]{3,2,1,0:T(8,128)(2,1)} %g_ref.3, bf16[768,1024]{1,0:T(8,128)(2,1)} %constant.68.clone.table, bf16[4,256,192]{2,1,0:T(8,128)(2,1)} %constant.69.clone.wh, ...), custom_call_target="tpu_custom_call" | custom-call | flops 5158993920 | bytes 8192000 | tf_op jit(solution)/shard_map/pallas_call | solution.py:248
  18.1 15.8 %shard_map.113 = f32[2,8,5,24,384]{4,3,2,1,0:T(8,128)} custom-call(s32[11]{0:T(128)} %pad_add_fusion.1.order, bf16[20,4,32,1024]{3,2,1,0:T(8,128)(2,1)} %f_ref.3, bf16[20,4,32,1024]{3,2,1,0:T(8,128)(2,1)} %g_ref.3, bf16[768,1024]{1,0:T(8,128)(2,1)} %constant.68.clone.table, bf16[4,256,192]{2,1,0:T(8,128)(2,1)} %constant.69.clone.wh, ...), custom_call_target="tpu_custom_call" | custom-call | flops 5158993920 | bytes 8192000 | tf_op jit(solution)/shard_map/pallas_call | solution.py:248
  34.0 1.7 fusion
  35.6 2.6 collective-permute-start.1
  38.3 33.0 %collective-permute-done.1 = f32[8,5,24,384]{3,2,1,0:T(8,128)S(1)} collective-permute-done((f32[8,5,24,384]{3,2,1,0:T(8,128)S(1)}, f32[8,5,24,384]{3,2,1,0:T(8,128)S(1)}, u32[]{:S(2)}, u32[]{:S(2)}) %collective-permute-start.1) | collective-permute-done | bytes 1474592 | tf_op jit(solution)/shard_map/ppermute | solution.py:276
  71.5 40.9 %all_to_all.20 = f32[8,5,24,384]{3,2,1,0:T(8,128)} all-to-all(f32[8,5,24,384]{3,2,1,0:T(8,128)S(1)} %fusion.2), channel_id=1, replica_groups=mesh['gx'=8,'gy'=4] {'gx'}, dimensions={0} | all-to-all | bytes 2949120 | tf_op jit(solution)/shard_map/all_to_all | solution.py:279
  112.4 10.0 %shard_map.115 = f32[4,120,576]{2,1,0:T(8,128)} custom-call(f32[8,120,384]{2,1,0:T(8,128)} %bitcast.31, bf16[8,192,1152]{2,1,0:T(8,128)(2,1)} %constant.71.clone.wh, bf16[8,192,1152]{2,1,0:T(8,128)(2,1)} %constant.72.clone.wl), custom_call_target="tpu_custom_call" | custom-call | tf_op jit(solution)/shard_map/pallas_call | solution.py:283
  122.4 2.7 copy.13
  125.1 3.5 %all-to-all-start.1 = ((f32[4,120,576]{1,2,0:T(8,128)}), f32[4,120,576]{1,2,0:T(8,128)S(1)}, u32[]{:S(2)}, u32[]{:S(2)}) async-start(f32[4,120,576]{1,2,0:T(8,128)} %copy.13), calls=%async_computation.1 | async-start | bytes 2359296 | tf_op jit(solution)/shard_map/all_to_all | solution.py:292
  129.4 15.1 %all-to-all-done.1 = f32[4,120,576]{1,2,0:T(8,128)S(1)} async-done(((f32[4,120,576]{1,2,0:T(8,128)}), f32[4,120,576]{1,2,0:T(8,128)S(1)}, u32[]{:S(2)}, u32[]{:S(2)}) %all-to-all-start.1) | async-done | bytes 1105952 | tf_op jit(solution)/shard_map/all_to_all | solution.py:292
  144.5 1.5 copy.14
  145.9 35.6 %shard_map.116 = (f32[20,24,288]{2,1,0:T(8,128)}, f32[2,2,20,6,24,128]{5,4,3,2,1,0:T(8,128)}, f32[2,20,6,24,128]{4,3,2,1,0:T(8,128)}) custom-call(f32[20,24,576]{2,1,0:T(8,128)} %bitcast.32, f32[24,576]{1,0:T(8,128)} %broadcast_select_fusion.w_ref, f32[2,20,20,6,24,24]{5,4,3,2,1,0:T(8,128)} %bitcast.30), custom_call_target="tpu_custom_call" | custom-call | flops 117964800 | bytes 58982400 | tf_op jit(solution)/shard_map/pallas_call | solution.py:303
  181.5 1.4 copy.15
  182.9 11.9 %all_to_all.21 = f32[4,120,288]{1,2,0:T(8,128)S(1)} all-to-all(f32[4,120,288]{1,2,0:T(8,128)S(1)} %copy.15), channel_id=1, replica_groups=mesh['gx'=8,'gy'=4] {'gy'}, dimensions={0} | all-to-all | bytes 1105920 | tf_op jit(solution)/shard_map/all_to_all | solution.py:325
  196.0 9.2 %shard_map.117 = f32[8,120,192]{2,1,0:T(8,128)} custom-call(f32[4,120,288]{2,1,0:T(8,128)} %copy.16.b_ref, bf16[8,192,1152]{2,1,0:T(8,128)(2,1)} %constant.71.clone.wh, bf16[8,192,1152]{2,1,0:T(8,128)(2,1)} %constant.72.clone.wl), custom_call_target="tpu_custom_call" | custom-call | tf_op jit(solution)/shard_map/pallas_call | solution.py:332
  205.2 2.6 copy.17
  207.8 4.2 %all-to-all-start.3 = ((f32[8,120,192]{1,2,0:T(8,128)}), f32[8,120,192]{1,2,0:T(8,128)}, u32[]{:S(2)}, u32[]{:S(2)}) async-start(f32[8,120,192]{1,2,0:T(8,128)} %copy.17), calls=%async_computation.3 | async-start | bytes 1572864 | tf_op jit(solution)/shard_map/all_to_all | solution.py:341
  212.0 1.8 slice_bitcast_fusion.3
  213.8 4.9 %slice_bitcast_fusion.1 = (f32[2,24,20,6,24]{4,1,3,2,0:T(8,128)S(1)}, f32[2,24,20,6,24]{4,1,3,2,0:T(8,128)}) fusion(f32[2,2,20,6,24,128]{5,4,3,2,1,0:T(8,128)} %get-tuple-element.8), kind=kLoop, calls=%fused_computation.2 | loop fusion | bytes 2211840 | tf_op jit(solution)/shard_map/mul | solution.py:329
  218.6 13.7 %all-to-all-done.3 = f32[8,120,192]{1,2,0:T(8,128)} async-done(((f32[8,120,192]{1,2,0:T(8,128)}), f32[8,120,192]{1,2,0:T(8,128)}, u32[]{:S(2)}, u32[]{:S(2)}) %all-to-all-start.3) | async-done | bytes 737312 | tf_op jit(solution)/shard_map/all_to_all | solution.py:341
  232.4 2.4 copy.18
  235.1 24.4 %multiply_add_fusion = f32[2,24,20,20,6,24]{5,1,4,3,2,0:T(8,128)} fusion(f32[24,20,6,24]{3,0,2,1:T(8,128)} %get-tuple-element.15, f32[2,24,20,6,24]{4,1,3,2,0:T(8,128)} %get-tuple-element.13, f32[24,20,6,24]{3,0,2,1:T(8,128)} %get-tuple-element.14, f32[2,24,20,6,24]{4,1,3,2,0:T(8,128)S(1)} %get-tuple-element.12), kind=kLoop, calls=%fused_computation | loop fusion | flops 8294400 | bytes 12718080 | tf_op jit(solution)/shard_map/add | solution.py:329
  263.1 14.2 %shard_map.118.rest_0_ = bf16[20,4,32,1024]{3,2,1,0:T(8,128)(2,1)} custom-call(s32[11]{0:T(128)} %pad_add_fusion.1.order, f32[2,8,5,24,192]{4,3,2,1,0:T(8,128)} %copy-done.4, bf16[384,1024]{1,0:T(8,128)(2,1)} %constant.73.clone.th, bf16[384,1024]{1,0:T(8,128)(2,1)} %constant.74.clone.tl, bf16[4,256,192]{2,1,0:T(8,128)(2,1)} %constant.69.clone.wh, ...), custom_call_target="tpu_custom_call" | custom-call | flops 3586129920 | bytes 4096000 | tf_op jit(solution)/shard_map/pallas_call | solution.py:359
  278.6 14.2 %shard_map.119 = bf16[20,4,32,1024]{3,2,1,0:T(8,128)(2,1)} custom-call(s32[11]{0:T(128)} %pad_add_fusion.order, f32[2,8,5,24,192]{4,3,2,1,0:T(8,128)} %copy-done.3, bf16[384,1024]{1,0:T(8,128)(2,1)} %constant.73.clone.th, bf16[384,1024]{1,0:T(8,128)(2,1)} %constant.74.clone.tl, ...), custom_call_target="tpu_custom_call", output_to_operand_aliasing={{}: (6, {})} | custom-call | flops 3586129920 | bytes 4096000 | tf_op jit(solution)/shard_map/pallas_call | solution.py:359
  (28 shorter events, 9.0 us)
Async XLA Ops:
  17.1 16.8 %collective-permute-start = (f32[2,8,5,24,384]{4,3,2,1,0:T(8,128)}, f32[2,8,5,24,384]{4,3,2,1,0:T(8,128)S(1)}, u32[]{:S(2)}, u32[]{:S(2)}) collective-permute-start(f32[2,8,5,24,384]{4,3,2,1,0:T(8,128)} %shard_map.114), channel_id=1, source_target_pairs={{0,1},{1,0},{2,3},{3,2},{4,5},{5,4},{6,7},{7,6},{8,9},{9,8},{10,11... | collective-permute-start | bytes 8847368 | tf_op jit(solution)/shard_map/ppermute | solution.py:274
  34.0 37.3 %copy-start.2 = (f32[2,8,5,24,384]{4,3,2,1,0:T(8,128)S(1)}, f32[2,8,5,24,384]{4,3,2,1,0:T(8,128)}, u32[]{:S(2)}) copy-start(f32[2,8,5,24,384]{4,3,2,1,0:T(8,128)} %shard_map.113) | copy-start | bytes 8847364
  35.6 35.6 %collective-permute-start.1 = (f32[8,5,24,384]{3,2,1,0:T(8,128)S(1)}, f32[8,5,24,384]{3,2,1,0:T(8,128)S(1)}, u32[]{:S(2)}, u32[]{:S(2)}) collective-permute-start(f32[8,5,24,384]{3,2,1,0:T(8,128)S(1)} %fusion), channel_id=1, source_target_pairs={{0,2},{1,3},{2,0},{3,1},{4,6},{5,7},{6,4},{7,5},{8,10},{9,11},{10,... | collective-permute-start | bytes 4423688 | tf_op jit(solution)/shard_map/ppermute | solution.py:276
  125.1 19.4 %all-to-all-start.1 = ((f32[4,120,576]{1,2,0:T(8,128)}), f32[4,120,576]{1,2,0:T(8,128)S(1)}, u32[]{:S(2)}, u32[]{:S(2)}) async-start(f32[4,120,576]{1,2,0:T(8,128)} %copy.13), calls=%async_computation.1 | async-start | bytes 2359296 | tf_op jit(solution)/shard_map/all_to_all | solution.py:292
  205.2 6.8 %copy-start.1 = (f32[2,20,6,24,128]{4,3,2,1,0:T(8,128)S(1)}, f32[2,20,6,24,128]{4,3,2,1,0:T(8,128)}, u32[]{:S(2)}) copy-start(f32[2,20,6,24,128]{4,3,2,1,0:T(8,128)} %get-tuple-element.9) | copy-start | bytes 8847364
  207.8 24.6 %all-to-all-start.3 = ((f32[8,120,192]{1,2,0:T(8,128)}), f32[8,120,192]{1,2,0:T(8,128)}, u32[]{:S(2)}, u32[]{:S(2)}) async-start(f32[8,120,192]{1,2,0:T(8,128)} %copy.17), calls=%async_computation.3 | async-start | bytes 1572864 | tf_op jit(solution)/shard_map/all_to_all | solution.py:341
  234.8 24.7 %collective-permute-start.2 = (f32[8,5,24,192]{3,2,1,0:T(8,128)}, f32[8,5,24,192]{3,2,1,0:T(8,128)S(1)}, u32[]{:S(2)}, u32[]{:S(2)}) collective-permute-start(f32[8,5,24,192]{3,2,1,0:T(8,128)} %bitcast.33), channel_id=1, source_target_pairs={{0,2},{1,3},{2,0},{3,1},{4,6},{5,7},{6,4},{7,5},{8,10},{9,11},{10,... | collective-permute-start | bytes 2211848 | tf_op jit(solution)/shard_map/ppermute | solution.py:343
  235.1 25.4 %copy-start = (f32[8,120,192]{2,1,0:T(8,128)S(1)}, f32[8,120,192]{2,1,0:T(8,128)}, u32[]{:S(2)}) copy-start(f32[8,120,192]{2,1,0:T(8,128)} %copy.18) | copy-start | bytes 2211844
  259.5 0.9 copy-start.5
  261.8 1.3 copy-start.4
  261.8 15.5 %collective-permute-start.3 = (f32[2,8,5,24,192]{4,3,2,1,0:T(8,128)S(1)}, f32[2,8,5,24,192]{4,3,2,1,0:T(8,128)S(1)}, u32[]{:S(2)}, u32[]{:S(2)}) collective-permute-start(f32[2,8,5,24,192]{4,3,2,1,0:T(8,128)S(1)} %pad_maximum_fusion.q_ref), channel_id=1, source_target_pairs={{0,1},{1,0},{2,3},{3,2},{4,5},{5,4},{6,7},{7,6},{8,9},{9,8},{10,11... | collective-permute-start | bytes 4423688 | tf_op jit(solution)/shard_map/ppermute | solution.py:346
  277.3 1.3 copy-start.3

commit v2 on v1

--- a/solution.py
+++ b/solution.py
@@ -270,11 +270,12 @@
     swap_core = [(d, d ^ 1) for d in range(groups)]
     swap_y = [(d, d ^ 2) for d in range(groups)]
 
-    away = forward(far)
-    arrived = lax.ppermute(away, "gy", swap_core)
-    kept = forward(near)
-    passed = lax.ppermute(kept[1] + arrived[1], "gy", swap_y)
-    summed = (kept[0] + arrived[0]) + passed
+    across = forward(order_of(me ^ 2, me ^ 3))
+    for_y = across[0] + lax.ppermute(across[1], "gy", swap_core)
+    for_y, here_order = lax.optimization_barrier((for_y, order_of(me, me ^ 1)))
+    passed = lax.ppermute(for_y, "gy", swap_y)
+    here = forward(here_order)
+    summed = (here[0] + lax.ppermute(here[1], "gy", swap_core)) + passed
 
     section = lax.all_to_all(summed, "gx", split_axis=0, concat_axis=0, tiled=True)
     rows = c_local * m_local

time: 294 us -> 283 us (0.963)
  waiting for transfers between devices: 61.8 us -> 46.5 us
  local copies, waits for them, and re-layouts: 21.8 us -> 25 us
    ppermute x2 -> x3, waiting for transfers between devices: 33 us -> 17.7 us  [the longest x1 15.1 us: per_device(): passed = lax.ppermute(for_y, 'gy', swap_y)]
    squeeze x0 -> x2, local copies, waits for them, and re-layouts: none -> 4.34 us  [the longest x1 2.73 us: per_device(): for_y = across[0] + lax.ppermute(across[1], 'gy', swap_core)]
  transfers between devices with their start and end apart: 6 -> 7, of which waited for: 3 -> 4; matrix products, arithmetic and copies ran while one was open for 11% -> 13% of each run, Pallas kernels for 10% -> 11%
where the time goes in v2:
time: 283 us; the launch traced here: 282 us
  Pallas kernels  115 us (41%)
  blocking collectives  52.6 us (19%)
  waiting for transfers between devices  46.5 us (16%)
  other arithmetic  31 us (11%)
  local copies, waits for them, and re-layouts  25 us (9%)
  starting transfers between devices  11.5 us (4%)
    all_to_all x1, blocking collectives, per_device(): lax.all_to_all(summed, 'gx', split_axis=0, concat_axis=0, tiled=True)  40.6 us
    pallas_call x1, Pallas kernels, per_device(): pl.pallas_call(back_kernel, out_shape=[jax.ShapeDtypeStruct((channels, m_...  35.6 us
    pallas_call x2, Pallas kernels, forward(): pl.pallas_call(functools.partial(zt_y_kernel, m_local), out_shape=jax.Sha...  31.6 us
    pallas_call x2, Pallas kernels, inverse(): pl.pallas_call(y_zt_back_kernel, out_shape=jax.ShapeDtypeStruct(field_in....  28.4 us
    add x1, other arithmetic, per_device(): grad_weight = left[0] * dual[0] + left[1] * dual[1]  24.4 us
    all_to_all x1, waiting for transfers between devices, per_device(): modes = lax.all_to_all(at_kx, 'gy', split_axis=0, concat_axis=0, tiled=True)  15.1 us
    ppermute x1, waiting for transfers between devices, per_device(): passed = lax.ppermute(for_y, 'gy', swap_y)  15.1 us
    all_to_all x1, waiting for transfers between devices, per_device(): own = lax.all_to_all(planes, 'gx', split_axis=0, concat_axis=0, tiled=True)  13.7 us
  transfers between devices with their start and end apart: 7, of which 4 were waited for; matrix products, arithmetic and copies ran while one was open for 13% of the time, Pallas kernels for 11%

profile of v2, /device:TPU:0, one launch (start us, length us, event | category | flops | bytes accessed | tf_op | source)
XLA Modules:
  0.0 282.1 jit_solution(2504441466455689613)
XLA Ops:
  1.2 15.8 %shard_map.113 = f32[2,8,5,24,384]{4,3,2,1,0:T(8,128)} custom-call(s32[11]{0:T(128)} %pad_add_fusion.1.order, bf16[20,4,32,1024]{3,2,1,0:T(8,128)(2,1)} %f_ref.3, bf16[20,4,32,1024]{3,2,1,0:T(8,128)(2,1)} %g_ref.3, bf16[768,1024]{1,0:T(8,128)(2,1)} %constant.74.clone.table, bf16[4,256,192]{2,1,0:T(8,128)(2,1)} %constant.75.clone.wh, ...), custom_call_target="tpu_custom_call" | custom-call | flops 5158993920 | bytes 8192000 | tf_op jit(solution)/shard_map/pallas_call | solution.py:248
  17.1 2.7 slice_bitcast_fusion.4
  20.9 2.6 collective-permute-done
  25.0 3.0 %collective-permute-start.2 = (f32[8,5,24,384]{3,2,1,0:T(8,128)S(1)}, f32[8,5,24,384]{3,2,1,0:T(8,128)S(1)}, u32[]{:S(2)}, u32[]{:S(2)}) collective-permute-start(f32[8,5,24,384]{3,2,1,0:T(8,128)S(1)} %fusion.2), channel_id=1, source_target_pairs={{0,2},{1,3},{2,0},{3,1},{4,6},{5,7},{6,4},{7,5},{8,10},{9,11},{10,... | collective-permute-start | bytes 4423688 | tf_op jit(solution)/shard_map/ppermute | solution.py:276
  28.0 15.8 %shard_map.114 = f32[2,8,5,24,384]{4,3,2,1,0:T(8,128)} custom-call(s32[11]{0:T(128)} %pad_add_fusion.2.order, bf16[20,4,32,1024]{3,2,1,0:T(8,128)(2,1)} %f_ref.3, bf16[20,4,32,1024]{3,2,1,0:T(8,128)(2,1)} %g_ref.3, bf16[768,1024]{1,0:T(8,128)(2,1)} %constant.74.clone.table, bf16[4,256,192]{2,1,0:T(8,128)(2,1)} %constant.75.clone.wh, ...), custom_call_target="tpu_custom_call" | custom-call | flops 5158993920 | bytes 8192000 | tf_op jit(solution)/shard_map/pallas_call | solution.py:248
  43.8 1.6 slice_bitcast_fusion.2
  45.5 15.1 %collective-permute-done.2 = f32[8,5,24,384]{3,2,1,0:T(8,128)S(1)} collective-permute-done((f32[8,5,24,384]{3,2,1,0:T(8,128)S(1)}, f32[8,5,24,384]{3,2,1,0:T(8,128)S(1)}, u32[]{:S(2)}, u32[]{:S(2)}) %collective-permute-start.2) | collective-permute-done | bytes 1474592 | tf_op jit(solution)/shard_map/ppermute | solution.py:276
  60.9 40.6 %all_to_all.20 = f32[8,5,24,384]{3,2,1,0:T(8,128)} all-to-all(f32[8,5,24,384]{3,2,1,0:T(8,128)S(1)} %fusion.1), channel_id=1, replica_groups=mesh['gx'=8,'gy'=4] {'gx'}, dimensions={0} | all-to-all | bytes 2949120 | tf_op jit(solution)/shard_map/all_to_all | solution.py:280
  101.5 10.0 %shard_map.115 = f32[4,120,576]{2,1,0:T(8,128)} custom-call(f32[8,120,384]{2,1,0:T(8,128)} %bitcast.39, bf16[8,192,1152]{2,1,0:T(8,128)(2,1)} %constant.77.clone.wh, bf16[8,192,1152]{2,1,0:T(8,128)(2,1)} %constant.78.clone.wl), custom_call_target="tpu_custom_call" | custom-call | tf_op jit(solution)/shard_map/pallas_call | solution.py:284
  111.4 2.7 copy.13
  114.1 3.5 %all-to-all-start.1 = ((f32[4,120,576]{1,2,0:T(8,128)}), f32[4,120,576]{1,2,0:T(8,128)S(1)}, u32[]{:S(2)}, u32[]{:S(2)}) async-start(f32[4,120,576]{1,2,0:T(8,128)} %copy.13), calls=%async_computation.1 | async-start | bytes 2359296 | tf_op jit(solution)/shard_map/all_to_all | solution.py:293
  118.4 15.1 %all-to-all-done.1 = f32[4,120,576]{1,2,0:T(8,128)S(1)} async-done(((f32[4,120,576]{1,2,0:T(8,128)}), f32[4,120,576]{1,2,0:T(8,128)S(1)}, u32[]{:S(2)}, u32[]{:S(2)}) %all-to-all-start.1) | async-done | bytes 1105952 | tf_op jit(solution)/shard_map/all_to_all | solution.py:293
  135.0 35.6 %shard_map.116 = (f32[20,24,288]{2,1,0:T(8,128)}, f32[2,2,20,6,24,128]{5,4,3,2,1,0:T(8,128)}, f32[2,20,6,24,128]{4,3,2,1,0:T(8,128)}) custom-call(f32[20,24,576]{2,1,0:T(8,128)} %bitcast.40, f32[24,576]{1,0:T(8,128)} %broadcast_select_fusion.w_ref, f32[2,20,20,6,24,24]{5,4,3,2,1,0:T(8,128)} %bitcast.38), custom_call_target="tpu_custom_call" | custom-call | flops 117964800 | bytes 58982400 | tf_op jit(solution)/shard_map/pallas_call | solution.py:304
  172.0 11.9 %all_to_all.21 = f32[4,120,288]{1,2,0:T(8,128)S(1)} all-to-all(f32[4,120,288]{1,2,0:T(8,128)S(1)} %copy.15), channel_id=1, replica_groups=mesh['gx'=8,'gy'=4] {'gy'}, dimensions={0} | all-to-all | bytes 1105920 | tf_op jit(solution)/shard_map/all_to_all | solution.py:326
  185.1 9.2 %shard_map.117 = f32[8,120,192]{2,1,0:T(8,128)} custom-call(f32[4,120,288]{2,1,0:T(8,128)} %copy.16.b_ref, bf16[8,192,1152]{2,1,0:T(8,128)(2,1)} %constant.77.clone.wh, bf16[8,192,1152]{2,1,0:T(8,128)(2,1)} %constant.78.clone.wl), custom_call_target="tpu_custom_call" | custom-call | tf_op jit(solution)/shard_map/pallas_call | solution.py:333
  194.3 2.6 copy.17
  196.8 4.2 %all-to-all-start.3 = ((f32[8,120,192]{1,2,0:T(8,128)}), f32[8,120,192]{1,2,0:T(8,128)}, u32[]{:S(2)}, u32[]{:S(2)}) async-start(f32[8,120,192]{1,2,0:T(8,128)} %copy.17), calls=%async_computation.3 | async-start | bytes 1572864 | tf_op jit(solution)/shard_map/all_to_all | solution.py:342
  201.1 1.8 slice_bitcast_fusion.7
  202.8 4.9 %slice_bitcast_fusion.1 = (f32[2,24,20,6,24]{4,1,3,2,0:T(8,128)S(1)}, f32[2,24,20,6,24]{4,1,3,2,0:T(8,128)}) fusion(f32[2,2,20,6,24,128]{5,4,3,2,1,0:T(8,128)} %get-tuple-element.12), kind=kLoop, calls=%fused_computation.2 | loop fusion | bytes 2211840 | tf_op jit(solution)/shard_map/mul | solution.py:330
  207.7 13.7 %all-to-all-done.3 = f32[8,120,192]{1,2,0:T(8,128)} async-done(((f32[8,120,192]{1,2,0:T(8,128)}), f32[8,120,192]{1,2,0:T(8,128)}, u32[]{:S(2)}, u32[]{:S(2)}) %all-to-all-start.3) | async-done | bytes 737312 | tf_op jit(solution)/shard_map/all_to_all | solution.py:342
  221.4 2.4 copy.18
  224.1 24.4 %multiply_add_fusion = f32[2,24,20,20,6,24]{5,1,4,3,2,0:T(8,128)} fusion(f32[24,20,6,24]{3,0,2,1:T(8,128)} %get-tuple-element.19, f32[2,24,20,6,24]{4,1,3,2,0:T(8,128)} %get-tuple-element.17, f32[24,20,6,24]{3,0,2,1:T(8,128)} %get-tuple-element.18, f32[2,24,20,6,24]{4,1,3,2,0:T(8,128)S(1)} %get-tuple-element.16), kind=kLoop, calls=%fused_computation | loop fusion | flops 8294400 | bytes 12718080 | tf_op jit(solution)/shard_map/add | solution.py:330
  252.4 14.2 %shard_map.118.rest_0_ = bf16[20,4,32,1024]{3,2,1,0:T(8,128)(2,1)} custom-call(s32[11]{0:T(128)} %pad_add_fusion.3.order, f32[2,8,5,24,192]{4,3,2,1,0:T(8,128)} %copy-done.5, bf16[384,1024]{1,0:T(8,128)(2,1)} %constant.79.clone.th, bf16[384,1024]{1,0:T(8,128)(2,1)} %constant.80.clone.tl, bf16[4,256,192]{2,1,0:T(8,128)(2,1)} %constant.75.clone.wh, ...), custom_call_target="tpu_custom_call" | custom-call | flops 3586129920 | bytes 4096000 | tf_op jit(solution)/shard_map/pallas_call | solution.py:360
  267.9 14.2 %shard_map.119 = bf16[20,4,32,1024]{3,2,1,0:T(8,128)(2,1)} custom-call(s32[11]{0:T(128)} %pad_add_fusion.order, f32[2,8,5,24,192]{4,3,2,1,0:T(8,128)} %copy-done.4, bf16[384,1024]{1,0:T(8,128)(2,1)} %constant.79.clone.th, bf16[384,1024]{1,0:T(8,128)(2,1)} %constant.80.clone.tl, ...), custom_call_target="tpu_custom_call", output_to_operand_aliasing={{}: (6, {})} | custom-call | flops 3586129920 | bytes 4096000 | tf_op jit(solution)/shard_map/pallas_call | solution.py:360
  (38 shorter events, 13.7 us)
Async XLA Ops:
  17.0 6.4 %copy-start.3 = (f32[2,8,5,24,384]{4,3,2,1,0:T(8,128)S(1)}, f32[2,8,5,24,384]{4,3,2,1,0:T(8,128)}, u32[]{:S(2)}) copy-start(f32[2,8,5,24,384]{4,3,2,1,0:T(8,128)} %shard_map.113) | copy-start | bytes 8847364
  19.8 3.7 %collective-permute-start = (f32[8,5,24,384]{3,2,1,0:T(8,128)}, f32[8,5,24,384]{3,2,1,0:T(8,128)}, u32[]{:S(2)}, u32[]{:S(2)}) collective-permute-start(f32[8,5,24,384]{3,2,1,0:T(8,128)} %slice_bitcast_fusion.4), channel_id=1, source_target_pairs={{0,1},{1,0},{2,3},{3,2},{4,5},{5,4},{6,7},{7,6},{8,9},{9,8},{10,11... | collective-permute-start | bytes 4423688 | tf_op jit(solution)/shard_map/ppermute | solution.py:274
  25.0 35.5 %collective-permute-start.2 = (f32[8,5,24,384]{3,2,1,0:T(8,128)S(1)}, f32[8,5,24,384]{3,2,1,0:T(8,128)S(1)}, u32[]{:S(2)}, u32[]{:S(2)}) collective-permute-start(f32[8,5,24,384]{3,2,1,0:T(8,128)S(1)} %fusion.2), channel_id=1, source_target_pairs={{0,2},{1,3},{2,0},{3,1},{4,6},{5,7},{6,4},{7,5},{8,10},{9,11},{10,... | collective-permute-start | bytes 4423688 | tf_op jit(solution)/shard_map/ppermute | solution.py:276
  43.8 16.8 %copy-start.2 = (f32[2,8,5,24,384]{4,3,2,1,0:T(8,128)S(1)}, f32[2,8,5,24,384]{4,3,2,1,0:T(8,128)}, u32[]{:S(2)}) copy-start(f32[2,8,5,24,384]{4,3,2,1,0:T(8,128)} %shard_map.114) | copy-start | bytes 8847364
  45.4 15.2 %collective-permute-start.1 = (f32[8,5,24,384]{3,2,1,0:T(8,128)S(1)}, f32[8,5,24,384]{3,2,1,0:T(8,128)S(1)}, u32[]{:S(2)}, u32[]{:S(2)}) collective-permute-start(f32[8,5,24,384]{3,2,1,0:T(8,128)S(1)} %slice_bitcast_fusion.2), channel_id=1, source_target_pairs={{0,1},{1,0},{2,3},{3,2},{4,5},{5,4},{6,7},{7,6},{8,9},{9,8},{10,11... | collective-permute-start | bytes 4423688 | tf_op jit(solution)/shard_map/ppermute | solution.py:278
  114.1 19.4 %all-to-all-start.1 = ((f32[4,120,576]{1,2,0:T(8,128)}), f32[4,120,576]{1,2,0:T(8,128)S(1)}, u32[]{:S(2)}, u32[]{:S(2)}) async-start(f32[4,120,576]{1,2,0:T(8,128)} %copy.13), calls=%async_computation.1 | async-start | bytes 2359296 | tf_op jit(solution)/shard_map/all_to_all | solution.py:293
  194.3 6.8 %copy-start.1 = (f32[2,20,6,24,128]{4,3,2,1,0:T(8,128)S(1)}, f32[2,20,6,24,128]{4,3,2,1,0:T(8,128)}, u32[]{:S(2)}) copy-start(f32[2,20,6,24,128]{4,3,2,1,0:T(8,128)} %get-tuple-element.13) | copy-start | bytes 8847364
  196.8 24.6 %all-to-all-start.3 = ((f32[8,120,192]{1,2,0:T(8,128)}), f32[8,120,192]{1,2,0:T(8,128)}, u32[]{:S(2)}, u32[]{:S(2)}) async-start(f32[8,120,192]{1,2,0:T(8,128)} %copy.17), calls=%async_computation.3 | async-start | bytes 1572864 | tf_op jit(solution)/shard_map/all_to_all | solution.py:342
  223.8 24.7 %collective-permute-start.3 = (f32[8,5,24,192]{3,2,1,0:T(8,128)}, f32[8,5,24,192]{3,2,1,0:T(8,128)S(1)}, u32[]{:S(2)}, u32[]{:S(2)}) collective-permute-start(f32[8,5,24,192]{3,2,1,0:T(8,128)} %bitcast.41), channel_id=1, source_target_pairs={{0,2},{1,3},{2,0},{3,1},{4,6},{5,7},{6,4},{7,5},{8,10},{9,11},{10,... | collective-permute-start | bytes 2211848 | tf_op jit(solution)/shard_map/ppermute | solution.py:344
  224.1 25.4 %copy-start = (f32[8,120,192]{2,1,0:T(8,128)S(1)}, f32[8,120,192]{2,1,0:T(8,128)}, u32[]{:S(2)}) copy-start(f32[8,120,192]{2,1,0:T(8,128)} %copy.18) | copy-start | bytes 2211844
  248.5 0.9 copy-start.6
  250.8 1.6 copy-start.5
  250.8 15.8 %collective-permute-start.4 = (f32[2,8,5,24,192]{4,3,2,1,0:T(8,128)S(1)}, f32[2,8,5,24,192]{4,3,2,1,0:T(8,128)S(1)}, u32[]{:S(2)}, u32[]{:S(2)}) collective-permute-start(f32[2,8,5,24,192]{4,3,2,1,0:T(8,128)S(1)} %pad_maximum_fusion.q_ref), channel_id=1, source_target_pairs={{0,1},{1,0},{2,3},{3,2},{4,5},{5,4},{6,7},{7,6},{8,9},{9,8},{10,11... | collective-permute-start | bytes 4423688 | tf_op jit(solution)/shard_map/ppermute | solution.py:347
  266.6 1.3 copy-start.4
